TPU v7x, 32 devices: a whole 2x2x4 slice. The times are simulated.
32 devices in a mesh: groups: 2 (over y), mp: 16 (over z, x, core).
Axes of the slice: x: 2, y: 2, z: 4, core: 2. Of those that a mesh axis runs over, the one named last changes fastest.
Arguments:
- hidden_in: bfloat16 [128, 18432], P('groups', 'mp'), parts along dimension 0, may hold values from -128 to 128
- w_qkv: bfloat16 [16, 9216, 1600], P('mp'), may hold values from -0.046875 to 0.046875
- w_out: bfloat16 [16, 1536, 9216], P('mp'), may hold values from -0.3125 to 0.3125
- key_cache: bfloat16 [128, 1792, 256], P(('groups', 'mp')), parts along dimension 0, may hold values from -256 to 256
- value_cache: bfloat16 [128, 1792, 256], P(('groups', 'mp')), parts along dimension 0, may hold values from -6 to 6
- lengths: int32 [128], P(('groups', 'mp')), parts along dimension 0, may hold values from 1 to 1792, as said below
Outputs:
- outputs: bfloat16 [128, 18432], P('groups', 'mp'), parts along dimension 0
There are 2 independent parts, one for each index of `groups`. A program takes and returns all parts, laid end to end along the dimension named above; an argument that names none is the same for every part. Nothing has to cross between parts.
Inputs may be any that keep to these rules, and one draw needn't show every extreme that they name: `lengths`: every row has at least one cached token; in each part some row holds exactly 1792.
All inputs are finite; a program needn't handle non-finite values.
Results may differ from a plain program's by a relative error of at most 0.012.
The roundings to bfloat16 on the way count: a program that leaves them out, or rounds other values in their place, can miss the bound.
Values may be sent and summed in bfloat16 or wider, within the bound.
A program may use at most 192 MiB of HBM per device.

v0:
```python
import jax
import jax.numpy as jnp
from jax import lax
from jax.sharding import PartitionSpec as P

D = 18432
COL_BITS = 3


def swapped(value, axis, bit):
    mask = 2**bit
    pairs = [(source, source ^ mask) for source in range(lax.axis_size(axis))]
    return lax.ppermute(value, axis, pairs)


def rotate(vectors, angle_now):
    half_dim = vectors.shape[-1] // 2
    front_half = vectors[..., :half_dim]
    back_half = vectors[..., half_dim:]
    cosine = jnp.cos(angle_now)
    sine_part = jnp.sin(angle_now)
    return jnp.concatenate(
        [front_half * cosine - back_half * sine_part, back_half * cosine + front_half * sine_part],
        -1,
    )


def cache_scores(query_part, key_cache, lengths):
    row_count = query_part.shape[0]
    head_size = key_cache.shape[-1]
    head_count = query_part.shape[1] // head_size
    half_dim = head_size // 2
    frequency = 10000.0 ** (-jnp.arange(half_dim, dtype=jnp.float32) / half_dim)
    angle_now = lengths.astype(jnp.float32)[:, None] * frequency[None, :]
    queries = rotate(
        query_part.reshape(row_count, head_count, head_size), angle_now[:, None, :]
    ).astype(jnp.bfloat16)
    score_scale = 1.0 / jnp.sqrt(jnp.float32(head_size))
    scores = (
        jnp.einsum("bhd,btd->bht", queries, key_cache, preferred_element_type=jnp.float32)
        * score_scale
    )
    live_mask = jnp.arange(key_cache.shape[1])[None, None, :] < lengths[:, None, None]
    return (queries, angle_now, jnp.where(live_mask, scores, -1e30))


def finish(queries, angle_now, scores, keyval_part, value_cache):
    row_count, head_count, head_size = queries.shape
    new_key = rotate(keyval_part[:, :head_size], angle_now).astype(jnp.bfloat16)
    new_value = keyval_part[:, head_size:].astype(jnp.bfloat16)
    score_scale = 1.0 / jnp.sqrt(jnp.float32(head_size))
    own_score = (
        jnp.sum(queries.astype(jnp.float32) * new_key.astype(jnp.float32)[:, None, :], -1)
        * score_scale
    )
    largest = jnp.maximum(jnp.max(scores, -1), own_score)
    weights = jnp.exp(scores - largest[..., None])
    own_weight = jnp.exp(own_score - largest)
    denominator = jnp.sum(weights, -1) + own_weight
    blended = jnp.einsum(
        "bht,btd->bhd",
        weights.astype(jnp.bfloat16),
        value_cache,
        preferred_element_type=jnp.float32,
    )
    blended = (
        blended
        + own_weight.astype(jnp.bfloat16).astype(jnp.float32)[..., None]
        * new_value.astype(jnp.float32)[:, None, :]
    )
    return (
        (blended / denominator[..., None])
        .reshape(row_count, head_count * head_size)
        .astype(jnp.bfloat16)
    )


def gather_features(block):
    device_index = lax.axis_index("mp")
    gathered = block
    for bit_level in range(COL_BITS):
        incoming = swapped(gathered, "mp", bit_level)
        mine_bit = device_index >> bit_level & 1
        gathered = jnp.where(
            mine_bit == 1,
            jnp.concatenate([incoming, gathered], 1),
            jnp.concatenate([gathered, incoming], 1),
        )
    return gathered


def reduce_rows(partial_value, high_bits):
    device_index = lax.axis_index("mp")
    total = partial_value
    for bit_level in reversed(range(COL_BITS, COL_BITS + high_bits)):
        half_rows = total.shape[0] // 2
        keep_back = device_index >> bit_level & 1 == 1
        outgoing = jnp.where(keep_back, total[:half_rows], total[half_rows:])
        staying = jnp.where(keep_back, total[half_rows:], total[:half_rows])
        total = staying + swapped(outgoing, "mp", bit_level)
    return total


def slots_to_holders(slots):
    device_index = lax.axis_index("mp")
    slot_count, row_count, width = slots.shape
    for bit_level in range(COL_BITS):
        shaped = slots.reshape(slot_count >> bit_level + 1, 2, 1 << bit_level, row_count, width)
        mine_bit = device_index >> bit_level & 1
        front_slots = shaped[:, 0]
        back_slots = shaped[:, 1]
        outgoing = jnp.where(mine_bit == 1, front_slots, back_slots)
        incoming = swapped(outgoing, "mp", bit_level)
        new_front = jnp.where(mine_bit == 1, incoming, front_slots)
        new_back = jnp.where(mine_bit == 1, back_slots, incoming)
        slots = jnp.stack([new_front, new_back], 1).reshape(slot_count, row_count, width)
    return slots


def reduce_features(partial_value):
    device_index = lax.axis_index("mp")
    total = partial_value
    for bit_level in reversed(range(COL_BITS)):
        half_cols = total.shape[1] // 2
        keep_back = device_index >> bit_level & 1 == 1
        outgoing = jnp.where(keep_back, total[:, :half_cols], total[:, half_cols:])
        staying = jnp.where(keep_back, total[:, half_cols:], total[:, :half_cols])
        total = staying + swapped(outgoing, "mp", bit_level)
    return total


def shards(hidden_in, w_qkv, w_out, key_cache, value_cache, lengths):
    qkv_tile = w_qkv[0]
    out_tile = w_out[0]
    own_rows = key_cache.shape[0]
    head_size = key_cache.shape[2]
    tile_count = 1 << COL_BITS
    col_width = qkv_tile.shape[1]
    full_cols = col_width * tile_count
    width_q = full_cols - 2 * head_size
    head_width = out_tile.shape[0]
    high_bits = lax.axis_size("mp").bit_length() - 1 - COL_BITS
    device_index = lax.axis_index("mp")
    column_block = device_index & tile_count - 1
    wide_in = hidden_in.astype(jnp.float32)
    sums_local = jnp.sum(wide_in, 1)
    squares_local = jnp.sum(wide_in * wide_in, 1)
    ones_row = jnp.ones((1, qkv_tile.shape[0]), jnp.bfloat16)
    tile_columns = jnp.dot(ones_row, qkv_tile, preferred_element_type=jnp.float32)[0]
    columns_local = lax.dynamic_update_slice_in_dim(
        jnp.zeros((full_cols,), jnp.float32), tile_columns, column_block * col_width, 0
    )
    sums_all, squares_all, column_total = lax.psum((sums_local, squares_local, columns_local), "mp")
    first_row = device_index * own_rows
    row_sums = lax.dynamic_slice_in_dim(sums_all, first_row, own_rows)
    row_squares = lax.dynamic_slice_in_dim(squares_all, first_row, own_rows)
    row_mean = row_sums / D
    variance = row_squares / D - row_mean * row_mean
    inverse = lax.rsqrt(variance + 1e-05)
    feature_block = gather_features(hidden_in)
    partial_value = jnp.dot(feature_block, qkv_tile, preferred_element_type=jnp.float32)
    group_rows = reduce_rows(partial_value, high_bits)
    slots = group_rows.reshape(tile_count, own_rows, col_width)
    arrived = slots_to_holders(slots)
    raw_sums = jnp.transpose(arrived, (1, 0, 2)).reshape(own_rows, full_cols)
    projected = inverse[:, None] * (raw_sums - row_mean[:, None] * column_total[None, :])
    queries, angle_now, scores = cache_scores(projected[:, :width_q], key_cache, lengths)
    attended = finish(queries, angle_now, scores, projected[:, width_q:], value_cache)
    block_cols = lax.dynamic_slice_in_dim(
        lax.all_gather(attended, "mp", axis=0, tiled=True), column_block * head_width, head_width, 1
    )
    partial_out = jnp.dot(block_cols, out_tile, preferred_element_type=jnp.float32)
    outputs = reduce_features(partial_out)
    return outputs.astype(jnp.bfloat16)


def solution(mesh):
    placed = (
        P("groups", "mp"),
        P("mp", None, None),
        P("mp", None, None),
        P(("groups", "mp"), None, None),
        P(("groups", "mp"), None, None),
        P(("groups", "mp")),
    )
    return jax.shard_map(
        shards, mesh=mesh, in_specs=placed, out_specs=P("groups", "mp"), check_vma=False
    )
```

profile of v0, /device:TPU:0, one launch (start us, length us, event | category | flops | bytes accessed | tf_op | source)
XLA Modules:
  0.0 242.1 jit_solution(1077846959856325483)
XLA Ops:
  6.5 0.0 all-gather.3.cloned.1.call-start
  6.5 0.5 collective-permute-start
  7.0 1.2 collective-permute-done
  8.2 1.1 maximum_select_fusion.3
  9.3 2.9 %collective-permute-start.1 = (bf16[64,2304]{1,0:T(8,128)(2,1)S(1)}, bf16[64,2304]{1,0:T(8,128)(2,1)S(1)}, u32[]{:S(2)}, u32[]{:S(2)}) collective-permute-start(bf16[64,2304]{1,0:T(8,128)(2,1)S(1)} %maximum_select_fusion.3), channel_id=1, source_target_pairs={{0,2},{1,3},{2,0},{3,1},{4,6},{5,7},{6,4},{7,5},{8,10},{9,11},{10,... | collective-permute-start | bytes 884744 | tf_op jit(solution)/shard_map/ppermute | solution.py:13
  12.2 7.3 %collective-permute-done.1 = bf16[64,2304]{1,0:T(8,128)(2,1)S(1)} collective-permute-done((bf16[64,2304]{1,0:T(8,128)(2,1)S(1)}, bf16[64,2304]{1,0:T(8,128)(2,1)S(1)}, u32[]{:S(2)}, u32[]{:S(2)}) %collective-permute-start.1) | collective-permute-done | bytes 294944 | tf_op jit(solution)/shard_map/ppermute | solution.py:13
  19.5 0.1 maximum_select_fusion.2
  19.6 1.9 collective-permute-start.2
  21.5 13.4 %fusion.17 = f32[1600]{0:T(1024)S(1)} fusion(bf16[1,9216,1600]{1,2,0:T(8,128)(2,1)} %param.7), kind=kOutput, calls=%fused_computation.23 | convolution fusion | flops 29491200 | bytes 29497600 | tf_op jit(solution)/shard_map/dot_general | solution.py:149
  34.9 0.0 copy-start.2
  34.9 0.0 collective-permute-done.2
  35.0 13.8 %fusion.2 = f32[64,1600]{1,0:T(8,128)S(1)} fusion(bf16[1,9216,1600]{1,2,0:T(8,128)(2,1)} %param.7, bf16[64,4608]{1,0:T(8,128)(2,1)S(1)} %maximum_select_fusion.2, bf16[64,4608]{1,0:T(8,128)(2,1)S(1)} %collective-permute-done.2, pred[]{:T(512)S(6)} %eq.10), kind=kOutput, calls=%fused_computation.2 | convolution fusion | flops 1892745216 | bytes 31080448 | tf_op jit(solution)/shard_map/dot_general | solution.py:161
  48.7 0.0 copy-start.1
  48.8 2.7 %collective-permute-start.3 = (f32[32,1600]{1,0:T(8,128)S(1)}, f32[32,1600]{1,0:T(8,128)S(1)}, u32[]{:S(2)}, u32[]{:S(2)}) collective-permute-start(f32[32,1600]{1,0:T(8,128)S(1)} %slice_select_fusion.3), channel_id=1, source_target_pairs={{0,8},{1,9},{2,10},{3,11},{4,12},{5,13},{6,14},{7,15},{8,0},{9,1},... | collective-permute-start | bytes 614408 | tf_op jit(solution)/shard_map/ppermute | solution.py:13
  51.4 0.0 copy-done.2
  51.4 0.1 iota_compare_fusion
  51.5 0.3 dynamic_update_slice.3
  51.9 8.6 %collective-permute-done.3 = f32[32,1600]{1,0:T(8,128)S(1)} collective-permute-done((f32[32,1600]{1,0:T(8,128)S(1)}, f32[32,1600]{1,0:T(8,128)S(1)}, u32[]{:S(2)}, u32[]{:S(2)}) %collective-permute-start.3) | collective-permute-done | bytes 204832 | tf_op jit(solution)/shard_map/ppermute | solution.py:13
  60.5 0.1 reshape_reshape.7
  60.6 0.1 collective-permute-start.4
  60.7 0.0 copy-done.1
  60.7 0.1 fusion.22
  60.8 61.2 %all-reduce = (f32[12800]{0:T(1024)S(1)}, f32[64]{0:T(128)S(1)}, f32[64]{0:T(128)S(1)}) all-reduce(f32[12800]{0:T(1024)S(1)} %dynamic_update_slice.3, f32[64]{0:T(128)S(1)} %get-tuple-element.6, f32[64]{0:T(128)S(1)} %get-tuple-element.5), channel_id=1, replica_groups=mesh['groups'=2,'mp'=16] {'mp'}, use_global_device_ids=true, to_apply=%region_4.0 | all-reduce | flops 12928 | bytes 103424 | tf_op jit(solution)/shard_map/psum | solution.py:153
  122.0 0.0 collective-permute-done.4
  122.1 0.1 collective-permute-start.5
  122.2 0.1 add_rsqrt_fusion
  122.3 4.6 %collective-permute-done.5 = f32[2,2,4,1600]{3,2,0,1:T(4,128)S(1)} collective-permute-done((f32[2,2,4,1600]{3,2,0,1:T(4,128)S(1)}, f32[2,2,4,1600]{3,2,0,1:T(4,128)S(1)}, u32[]{:S(2)}, u32[]{:S(2)}) %collective-permute-start.5) | collective-permute-done | bytes 102432 | tf_op jit(solution)/shard_map/ppermute | solution.py:13
  126.9 0.1 select_bitcast_fusion.3
  127.0 0.1 pad_maximum_fusion
  127.1 0.1 collective-permute-start.6
  127.2 4.7 %collective-permute-done.6 = f32[1,4,4,1600]{3,2,1,0:T(4,128)S(1)} collective-permute-done((f32[1,4,4,1600]{3,2,1,0:T(4,128)S(1)}, f32[1,4,4,1600]{3,2,1,0:T(4,128)S(1)}, u32[]{:S(2)}, u32[]{:S(2)}) %collective-permute-start.6) | collective-permute-done | bytes 102432 | tf_op jit(solution)/shard_map/ppermute | solution.py:13
  131.9 0.1 pad_maximum_fusion.1
  132.0 0.1 reshape.174
  132.1 0.1 subtract_multiply_fusion
  132.3 0.1 subtract_convert_fusion.1
  132.5 0.1 multiply_reduce_fusion
  132.6 0.0 copy-start
  132.6 3.5 %fusion.38 = (f32[4,48]{1,0:T(4,128)S(1)}, f32[4,48,1792]{2,1,0:T(8,128)S(1)}) fusion(bf16[4,1792,256]{2,1,0:T(8,128)(2,1)} %param.9, bf16[4,48,128]{2,1,0:T(8,128)(2,1)S(1)} %get-tuple-element.19, bf16[4,48,128]{2,1,0:T(8,128)(2,1)S(1)} %get-tuple-element.18, pred[4,1792]{1,0:T(4,128)(4,1)S(1)} %iota_compare_fusion), kind=kOutput, calls=%fused_computation.85 | convolution fusion | flops 177389376 | bytes 5152512 | tf_op jit(solution)/shard_map/bhd,btd->bht/dot_general | solution.py:40
  136.1 0.3 fusion.7
  136.4 0.0 copy-done
  136.5 0.8 fusion.16
  137.3 0.7 reshape.176
  138.0 0.0 all-gather.3.cloned.1.call-update
  138.0 37.1 %all-gather.3.cloned.1.call-done = bf16[16,4,12288]{2,1,0:T(4,128)(2,1)} async-done(((bf16[1,4,12288]{2,1,0:T(4,128)(2,1)}), bf16[16,4,12288]{2,1,0:T(4,128)(2,1)}) %all-gather.3.cloned.1.call-update) | async-done | bytes 1572880 | tf_op jit(solution)/shard_map/all_gather | solution.py:170
  175.1 2.7 %reshape.177 = bf16[64,12288]{1,0:T(8,128)(2,1)S(1)} reshape(bf16[16,4,12288]{2,1,0:T(4,128)(2,1)} %all-gather.3.cloned.1.call-done) | data formatting | bytes 3145728
  177.8 11.6 %fusion.4 = f32[64,9216]{1,0:T(8,128)S(1)} fusion(bf16[1,1536,9216]{2,1,0:T(8,128)(2,1)} %param.8, bf16[64,12288]{1,0:T(8,128)(2,1)S(1)} %reshape.177, s32[]{:T(128)S(6)} %select_n.177), kind=kOutput, calls=%fused_computation.4 | convolution fusion | flops 1811939328 | bytes 30867460 | tf_op jit(solution)/shard_map/dot_general | solution.py:172
  189.4 0.1 slice_select_fusion
  189.5 0.5 collective-permute-start.7
  190.0 27.7 %collective-permute-done.7 = f32[64,4608]{1,0:T(8,128)S(1)} collective-permute-done((f32[64,4608]{1,0:T(8,128)S(1)}, f32[64,4608]{1,0:T(8,128)S(1)}, u32[]{:S(2)}, u32[]{:S(2)}) %collective-permute-start.7) | collective-permute-done | bytes 1179680 | tf_op jit(solution)/shard_map/ppermute | solution.py:13
  217.7 0.2 select_add_fusion
  217.9 0.1 slice_select_fusion.1
  218.0 0.7 collective-permute-start.8
  218.7 14.1 %collective-permute-done.8 = f32[64,2304]{1,0:T(8,128)S(1)} collective-permute-done((f32[64,2304]{1,0:T(8,128)S(1)}, f32[64,2304]{1,0:T(8,128)S(1)}, u32[]{:S(2)}, u32[]{:S(2)}) %collective-permute-start.8) | collective-permute-done | bytes 589856 | tf_op jit(solution)/shard_map/ppermute | solution.py:13
  232.8 0.1 select_add_fusion.1
  232.9 0.1 collective-permute-start.9
  233.0 1.6 collective-permute-done.9
  234.6 0.7 add_convert_fusion
  (19 shorter events, 0.4 us)
Async XLA Ops:
  6.5 168.5 %all-gather.3.cloned.1.call-start = ((), (), s32[]{:S(2)}) async-start(), calls=%async_computation | async-start | bytes 1671168 | tf_op jit(solution)/shard_map/all_gather | solution.py:170
  6.5 1.7 collective-permute-start
  9.3 10.2 %collective-permute-start.1 = (bf16[64,2304]{1,0:T(8,128)(2,1)S(1)}, bf16[64,2304]{1,0:T(8,128)(2,1)S(1)}, u32[]{:S(2)}, u32[]{:S(2)}) collective-permute-start(bf16[64,2304]{1,0:T(8,128)(2,1)S(1)} %maximum_select_fusion.3), channel_id=1, source_target_pairs={{0,2},{1,3},{2,0},{3,1},{4,6},{5,7},{6,4},{7,5},{8,10},{9,11},{10,... | collective-permute-start | bytes 884744 | tf_op jit(solution)/shard_map/ppermute | solution.py:13
  19.6 15.3 %collective-permute-start.2 = (bf16[64,4608]{1,0:T(8,128)(2,1)S(1)}, bf16[64,4608]{1,0:T(8,128)(2,1)S(1)}, u32[]{:S(2)}, u32[]{:S(2)}) collective-permute-start(bf16[64,4608]{1,0:T(8,128)(2,1)S(1)} %maximum_select_fusion.2), channel_id=1, source_target_pairs={{0,4},{1,5},{2,6},{3,7},{4,0},{5,1},{6,2},{7,3},{8,12},{9,13},{10,... | collective-permute-start | bytes 1769480 | tf_op jit(solution)/shard_map/ppermute | solution.py:13
  34.9 16.5 %copy-start.2 = (s32[4]{0:T(128)S(1)}, s32[4]{0:T(128)}, u32[]{:S(2)}) copy-start(s32[4]{0:T(128)} %param.11) | copy-start | bytes 52
  48.7 11.9 %copy-start.1 = (bf16[64,1152]{1,0:T(8,128)(2,1)S(1)}, bf16[64,1152]{1,0:T(8,128)(2,1)}, u32[]{:S(2)}) copy-start(bf16[64,1152]{1,0:T(8,128)(2,1)} %param.6) | copy-start | bytes 442372
  48.8 11.7 %collective-permute-start.3 = (f32[32,1600]{1,0:T(8,128)S(1)}, f32[32,1600]{1,0:T(8,128)S(1)}, u32[]{:S(2)}, u32[]{:S(2)}) collective-permute-start(f32[32,1600]{1,0:T(8,128)S(1)} %slice_select_fusion.3), channel_id=1, source_target_pairs={{0,8},{1,9},{2,10},{3,11},{4,12},{5,13},{6,14},{7,15},{8,0},{9,1},... | collective-permute-start | bytes 614408 | tf_op jit(solution)/shard_map/ppermute | solution.py:13
  60.6 61.4 %collective-permute-start.4 = (f32[4,1,4,1600]{3,2,0,1:T(4,128)S(1)}, f32[4,1,4,1600]{3,2,0,1:T(4,128)S(1)}, u32[]{:S(2)}, u32[]{:S(2)}) collective-permute-start(f32[4,1,4,1600]{3,2,0,1:T(4,128)S(1)} %fusion.28), channel_id=1, source_target_pairs={{0,1},{1,0},{2,3},{3,2},{4,5},{5,4},{6,7},{7,6},{8,9},{9,8},{10,11... | collective-permute-start | bytes 307208 | tf_op jit(solution)/shard_map/ppermute | solution.py:13
  122.1 4.8 %collective-permute-start.5 = (f32[2,2,4,1600]{3,2,0,1:T(4,128)S(1)}, f32[2,2,4,1600]{3,2,0,1:T(4,128)S(1)}, u32[]{:S(2)}, u32[]{:S(2)}) collective-permute-start(f32[2,2,4,1600]{3,2,0,1:T(4,128)S(1)} %broadcast_select_fusion), channel_id=1, source_target_pairs={{0,2},{1,3},{2,0},{3,1},{4,6},{5,7},{6,4},{7,5},{8,10},{9,11},{10,... | collective-permute-start | bytes 307208 | tf_op jit(solution)/shard_map/ppermute | solution.py:13
  127.1 4.8 %collective-permute-start.6 = (f32[1,4,4,1600]{3,2,1,0:T(4,128)S(1)}, f32[1,4,4,1600]{3,2,1,0:T(4,128)S(1)}, u32[]{:S(2)}, u32[]{:S(2)}) collective-permute-start(f32[1,4,4,1600]{3,2,1,0:T(4,128)S(1)} %fusion.30), channel_id=1, source_target_pairs={{0,4},{1,5},{2,6},{3,7},{4,0},{5,1},{6,2},{7,3},{8,12},{9,13},{10,... | collective-permute-start | bytes 307208 | tf_op jit(solution)/shard_map/ppermute | solution.py:13
  132.6 3.9 %copy-start = (bf16[4,1792,256]{2,1,0:T(8,128)(2,1)S(1)}, bf16[4,1792,256]{2,1,0:T(8,128)(2,1)}, u32[]{:S(2)}) copy-start(bf16[4,1792,256]{2,1,0:T(8,128)(2,1)} %param.10) | copy-start | bytes 11010052
  189.5 28.2 %collective-permute-start.7 = (f32[64,4608]{1,0:T(8,128)S(1)}, f32[64,4608]{1,0:T(8,128)S(1)}, u32[]{:S(2)}, u32[]{:S(2)}) collective-permute-start(f32[64,4608]{1,0:T(8,128)S(1)} %slice_select_fusion), channel_id=1, source_target_pairs={{0,4},{1,5},{2,6},{3,7},{4,0},{5,1},{6,2},{7,3},{8,12},{9,13},{10,... | collective-permute-start | bytes 3538952 | tf_op jit(solution)/shard_map/ppermute | solution.py:13
  218.0 14.7 %collective-permute-start.8 = (f32[64,2304]{1,0:T(8,128)S(1)}, f32[64,2304]{1,0:T(8,128)S(1)}, u32[]{:S(2)}, u32[]{:S(2)}) collective-permute-start(f32[64,2304]{1,0:T(8,128)S(1)} %slice_select_fusion.1), channel_id=1, source_target_pairs={{0,2},{1,3},{2,0},{3,1},{4,6},{5,7},{6,4},{7,5},{8,10},{9,11},{10,... | collective-permute-start | bytes 1769480 | tf_op jit(solution)/shard_map/ppermute | solution.py:13
  232.9 1.6 collective-permute-start.9
Sparse Core Ops, SparseCore 0:
  138.1 36.9 all-gather.2
where the time goes:
time: 242 us
  waiting for transfers between devices  107 us (44%)
  blocking collectives  61.2 us (25%)
  matrix products  43.1 us (18%)
  between operations  13.7 us (6%)
  starting transfers between devices  9.37 us (4%)
  local copies, waits for them, and re-layouts  3.98 us (2%)
  other arithmetic  3.94 us (2%)
    ppermute x10, waiting for transfers between devices, swapped(): return lax.ppermute(value, axis, pairs)  69.7 us
    psum x1, blocking collectives, shards(): lax.psum((sums_local, squares_local, columns_local), 'mp')  61.2 us
    all_gather x1, waiting for transfers between devices, shards(): lax.all_gather(attended, 'mp', axis=0, tiled=True)  37.1 us
    dot_general x1, matrix products, shards(): jnp.dot(feature_block, qkv_tile, preferred_element_type=jnp.float32)  13.8 us
    dot_general x1, matrix products, shards(): jnp.dot(ones_row, qkv_tile, preferred_element_type=jnp.float32)[0]  13.4 us
    dot_general x1, matrix products, shards(): jnp.dot(block_cols, out_tile, preferred_element_type=jnp.float32)  11.6 us
    ppermute x10, starting transfers between devices, swapped(): return lax.ppermute(value, axis, pairs)  9.37 us
  transfers between devices with their start and end apart: 11, of which 9 were waited for; matrix products, arithmetic and copies ran while one was open for 6% of the time, Pallas kernels for 0%

commit v1 on v0

--- a/solution.py
+++ b/solution.py
@@ -1,8 +1,11 @@
 import jax
 import jax.numpy as jnp
 from jax import lax
+from jax.experimental import pallas as pl
+from jax.experimental.pallas import tpu as pltpu
 from jax.sharding import PartitionSpec as P
 
+MESH = pl.DeviceIdType.MESH
 D = 18432
 COL_BITS = 3
 
@@ -129,7 +132,7 @@
     return total
 
 
-def shards(hidden_in, w_qkv, w_out, key_cache, value_cache, lengths):
+def shards_plain(hidden_in, w_qkv, w_out, key_cache, value_cache, lengths):
     qkv_tile = w_qkv[0]
     out_tile = w_out[0]
     own_rows = key_cache.shape[0]
@@ -174,6 +177,353 @@
     return outputs.astype(jnp.bfloat16)
 
 
+RING = 4
+
+
+def flipped(index, flips, bits):
+    total = 0
+    for level in range(bits):
+        own_bit = index // 2**level % 2
+        flip_bit = flips // 2**level % 2
+        total = total + (own_bit + flip_bit - 2 * own_bit * flip_bit) * 2**level
+    return total
+
+
+def block_kernel(
+    hid_ref, cos_ref, sin_ref, len_ref, wq_hbm, wo_hbm, key_hbm, val_hbm, out_ref,
+    xb, wb, acc, stat_send, stat_recv, psb, prb, pj, qf, attf, msgf, dsb, drb, lhsf, lhs,
+    keys, vals, wo, pbuf, erecv, irecv,
+    w_sem, kv_sem, wo_sem, xs_sem, xr_sem, ss_sem, sr_sem, ps_sem, pr_sem,
+    ds_sem, dr_sem, es_sem, er_sem, is_sem, ir_sem,
+):
+    me = lax.axis_index("mp")
+    low = me % 8
+    high = me // 8 * 8
+    part_rows, feats = hid_ref.shape
+    own_rows = cos_ref.shape[0]
+    col_width = acc.shape[1]
+    head_size = qf.shape[2]
+    head_count = qf.shape[1]
+    half_dim = head_size // 2
+    width_q = head_count * head_size
+    out_cols = wo.shape[2]
+    n_dev = 16
+
+    def w_copy(step, slot):
+        rows = pl.ds(pl.multiple_of(flipped(low, step, 3) * feats, feats), feats)
+        return pltpu.make_async_copy(wq_hbm.at[0, rows], wb.at[slot], w_sem.at[slot])
+
+    def wo_copy(block):
+        cols = pl.ds(block * out_cols, out_cols)
+        return pltpu.make_async_copy(wo_hbm.at[0, :, cols], wo.at[block], wo_sem.at[block])
+
+    key_copy = pltpu.make_async_copy(key_hbm, keys, kv_sem.at[0])
+    val_copy = pltpu.make_async_copy(val_hbm, vals, kv_sem.at[1])
+
+    for step in range(RING):
+        w_copy(step, step).start()
+
+    barrier = pltpu.get_barrier_semaphore()
+    for flips in range(1, n_dev):
+        pl.semaphore_signal(
+            barrier, inc=1, device_id={"mp": flipped(me, flips, 4)}, device_id_type=MESH
+        )
+    pl.semaphore_wait(barrier, n_dev - 1)
+
+    def x_copy(source, flips, slot):
+        return pltpu.make_async_remote_copy(
+            src_ref=source, dst_ref=xb.at[slot], send_sem=xs_sem.at[slot],
+            recv_sem=xr_sem.at[slot], device_id={"mp": high + flipped(low, flips, 3)},
+            device_id_type=MESH,
+        )
+
+    for flips in (2, 4, 6, 1):
+        x_copy(hid_ref, flips, flips).start()
+    xb[0] = hid_ref[...]
+    acc[...] = jnp.zeros_like(acc)
+
+    stat_copy = pltpu.make_async_remote_copy(
+        src_ref=stat_send, dst_ref=stat_recv, send_sem=ss_sem, recv_sem=sr_sem,
+        device_id={"mp": flipped(me, 8, 4)}, device_id_type=MESH,
+    )
+
+    def step_body(step, sums):
+        total, squares = sums
+        slot = step % RING
+
+        @pl.when(step > 0)
+        def _():
+            x_copy(xb.at[step], 1, step).wait_recv()
+
+        @pl.when((step >= 2) & (step % 2 == 0))
+        def _():
+            x_copy(xb.at[step], 1, step + 1).start()
+
+        features = xb[step]
+        wide = features.astype(jnp.float32)
+        total = total + jnp.sum(wide, 1, keepdims=True)
+        squares = squares + jnp.sum(wide * wide, 1, keepdims=True)
+
+        @pl.when(step == 7)
+        def _():
+            lane = lax.broadcasted_iota(jnp.int32, stat_send.shape, 1)
+            stat_send[...] = jnp.where(lane < 64, total, squares)
+            stat_copy.start()
+
+        w_copy(step, slot).wait()
+        with_ones = jnp.concatenate([features, jnp.ones((16, feats), jnp.bfloat16)], 0)
+        acc[...] += jnp.dot(with_ones, wb[slot], preferred_element_type=jnp.float32)
+
+        @pl.when(step + RING < 8)
+        def _():
+            w_copy(step + RING, slot).start()
+
+        @pl.when(step == 3)
+        def _():
+            key_copy.start()
+            val_copy.start()
+            for block in range(4):
+                wo_copy(block).start()
+
+        @pl.when(step == 5)
+        def _():
+            for block in range(4, 8):
+                wo_copy(block).start()
+
+        return (total, squares)
+
+    nothing = jnp.zeros((part_rows, 1), jnp.float32)
+    lax.fori_loop(0, 8, step_body, (nothing, nothing))
+    stat_copy.wait()
+    both = stat_send[...] + stat_recv[...]
+    row_mean = both[:, :1] / D
+    variance = both[:, 64:65] / D - row_mean * row_mean
+    inverse = lax.rsqrt(variance + 1e-05)
+    projected = inverse * (acc[:part_rows] - row_mean * acc[part_rows : part_rows + 1])
+    for dev in range(n_dev):
+        psb[dev] = projected[dev * own_rows : (dev + 1) * own_rows]
+
+    def p_copy(flips):
+        target = flipped(me, flips, 4)
+        return pltpu.make_async_remote_copy(
+            src_ref=psb.at[target], dst_ref=prb.at[me], send_sem=ps_sem.at[flips],
+            recv_sem=pr_sem.at[flips], device_id={"mp": target}, device_id_type=MESH,
+        )
+
+    def p_arrival(flips):
+        source = flipped(me, flips, 4)
+        return pltpu.make_async_remote_copy(
+            src_ref=psb.at[source], dst_ref=prb.at[source], send_sem=ps_sem.at[flips],
+            recv_sem=pr_sem.at[flips], device_id={"mp": source}, device_id_type=MESH,
+        )
+
+    for flips in range(n_dev - 1, 0, -1):
+        p_copy(flips).start()
+    prb[me] = psb[me]
+    for flips in range(1, n_dev):
+        p_arrival(flips).wait_recv()
+    for block in range(8):
+        pj[:, block * col_width : (block + 1) * col_width] = prb[block] + prb[block + 8]
+    for head in range(head_count):
+        for row in range(own_rows):
+            qf[row, head : head + 1, :] = pj[
+                row : row + 1, head * head_size : (head + 1) * head_size
+            ]
+
+    key_copy.wait()
+    val_copy.wait()
+    scale = 1.0 / 16.0 if head_size == 256 else head_size**-0.5
+
+    def turned(vectors, cosine, sine):
+        front, back = vectors[:, :half_dim], vectors[:, half_dim:]
+        return jnp.concatenate([front * cosine - back * sine, back * cosine + front * sine], 1)
+
+    for row in range(own_rows):
+        cosine, sine = cos_ref[row : row + 1], sin_ref[row : row + 1]
+        queries = turned(qf[row], cosine, sine).astype(jnp.bfloat16)
+        new_key = turned(pj[row : row + 1, width_q : width_q + head_size], cosine, sine)
+        new_key = new_key.astype(jnp.bfloat16).astype(jnp.float32)
+        new_value = pj[row : row + 1, width_q + head_size :]
+        new_value = new_value.astype(jnp.bfloat16).astype(jnp.float32)
+        scores = scale * lax.dot_general(
+            queries, keys[row], (((1,), (1,)), ((), ())), preferred_element_type=jnp.float32
+        )
+        slots = lax.broadcasted_iota(jnp.int32, scores.shape, 1)
+        scores = jnp.where(slots < len_ref[row : row + 1, :1], scores, -1e30)
+        own_score = scale * jnp.sum(queries.astype(jnp.float32) * new_key, 1, keepdims=True)
+        largest = jnp.maximum(jnp.max(scores, 1, keepdims=True), own_score)
+        weights = jnp.exp(scores - largest)
+        own_weight = jnp.exp(own_score - largest)
+        denominator = jnp.sum(weights, 1, keepdims=True) + own_weight
+        blended = jnp.dot(
+            weights.astype(jnp.bfloat16), vals[row], preferred_element_type=jnp.float32
+        )
+        blended = blended + own_weight.astype(jnp.bfloat16).astype(jnp.float32) * new_value
+        attf[row] = blended / denominator
+
+    parts = msgf.shape[1] // own_rows
+    tiles = msgf.shape[2] // 128
+    for block in range(8):
+        for part in range(parts):
+            for tile in range(tiles):
+                column = ((block * parts + part) * tiles + tile) * 128
+                head, lane = column // head_size, column % head_size
+                for row in range(own_rows):
+                    at = part * own_rows + row
+                    msgf[block, at : at + 1, tile * 128 : (tile + 1) * 128] = attf[
+                        row, head : head + 1, lane : lane + 128
+                    ]
+        dsb[block] = msgf[block].astype(jnp.bfloat16)
+
+    def d_copy(flips):
+        target = flipped(me, flips, 4)
+        return pltpu.make_async_remote_copy(
+            src_ref=dsb.at[target % 8], dst_ref=drb.at[me], send_sem=ds_sem.at[flips],
+            recv_sem=dr_sem.at[flips], device_id={"mp": target}, device_id_type=MESH,
+        )
+
+    def d_arrival(flips):
+        source = flipped(me, flips, 4)
+        return pltpu.make_async_remote_copy(
+            src_ref=dsb.at[source % 8], dst_ref=drb.at[source], send_sem=ds_sem.at[flips],
+            recv_sem=dr_sem.at[flips], device_id={"mp": source}, device_id_type=MESH,
+        )
+
+    for flips in range(n_dev - 1, 0, -1):
+        d_copy(flips).start()
+    drb[me] = dsb[low]
+    for flips in range(1, n_dev):
+        d_arrival(flips).wait_recv()
+    width = msgf.shape[2]
+    for dev in range(n_dev):
+        arrived = drb[dev].astype(jnp.float32)
+        for part in range(parts):
+            lhsf[dev * own_rows : (dev + 1) * own_rows, part * width : (part + 1) * width] = (
+                arrived[part * own_rows : (part + 1) * own_rows]
+            )
+    lhs[...] = lhsf[...].astype(jnp.bfloat16)
+    for block in range(8):
+        wo_copy(block).wait()
+
+    def e_copy(turn):
+        return pltpu.make_async_remote_copy(
+            src_ref=pbuf.at[2 * turn], dst_ref=erecv.at[turn], send_sem=es_sem.at[turn],
+            recv_sem=er_sem.at[turn], device_id={"mp": flipped(me, 1, 4)}, device_id_type=MESH,
+        )
+
+    def i_copy(turn):
+        return pltpu.make_async_remote_copy(
+            src_ref=pbuf.at[2 * turn + 1], dst_ref=irecv.at[turn], send_sem=is_sem.at[turn],
+            recv_sem=ir_sem.at[turn],
+            device_id={"mp": high + flipped(low, 6 - 2 * turn, 3)}, device_id_type=MESH,
+        )
+
+    def out_body(turn, carry):
+        flips = 6 - 2 * turn
+        pbuf[2 * turn] = jnp.dot(
+            lhs[...], wo[flipped(low, flips + 1, 3)], preferred_element_type=jnp.float32
+        )
+        e_copy(turn).start()
+        pbuf[2 * turn + 1] = jnp.dot(
+            lhs[...], wo[flipped(low, flips, 3)], preferred_element_type=jnp.float32
+        )
+        e_copy(turn).wait_recv()
+        pbuf[2 * turn + 1] += erecv[turn]
+
+        @pl.when(turn < 3)
+        def _():
+            i_copy(turn).start()
+
+        return carry
+
+    lax.fori_loop(0, 4, out_body, 0)
+    for turn in range(3):
+        i_copy(turn).wait_recv()
+    out_ref[...] = (pbuf[7] + irecv[0] + irecv[1] + irecv[2]).astype(jnp.bfloat16)
+
+    for slot in range(1, 8):
+        x_copy(hid_ref, 1, slot).wait_send()
+    for flips in range(1, n_dev):
+        p_copy(flips).wait_send()
+        d_copy(flips).wait_send()
+    for turn in range(4):
+        e_copy(turn).wait_send()
+    for turn in range(3):
+        i_copy(turn).wait_send()
+
+
+def shards(hidden_in, w_qkv, w_out, key_cache, value_cache, lengths):
+    part_rows, feats = hidden_in.shape
+    own_rows, slot_count, head_size = key_cache.shape
+    _, w_rows, col_width = w_qkv.shape
+    _, head_width, out_width = w_out.shape
+    if (
+        lax.axis_size("mp") != 16
+        or w_rows != 8 * feats
+        or own_rows != 4
+        or part_rows != 64
+        or feats % 128 != 0
+        or head_width % 512 != 0
+        or head_size != 256
+    ):
+        return shards_plain(hidden_in, w_qkv, w_out, key_cache, value_cache, lengths)
+    half_dim = head_size // 2
+    out_cols = out_width // 8
+    full_cols = col_width * 8
+    head_count = head_width * 8 // head_size
+    frequency = 10000.0 ** (-jnp.arange(half_dim, dtype=jnp.float32) / half_dim)
+    angle_now = lengths.astype(jnp.float32)[:, None] * frequency[None, :]
+    spread = jnp.broadcast_to(lengths[:, None], (own_rows, 128))
+    f32, bf16 = jnp.float32, jnp.bfloat16
+    dma = pltpu.SemaphoreType.DMA
+    in_vmem = pl.BlockSpec(memory_space=pltpu.VMEM)
+    anywhere = pl.BlockSpec(memory_space=pl.ANY)
+    return pl.pallas_call(
+        block_kernel,
+        out_shape=jax.ShapeDtypeStruct((part_rows, out_cols), bf16),
+        in_specs=[in_vmem] * 4 + [anywhere] * 4,
+        out_specs=in_vmem,
+        scratch_shapes=[
+            pltpu.VMEM((8, part_rows, feats), bf16),
+            pltpu.VMEM((RING, feats, col_width), bf16),
+            pltpu.VMEM((part_rows + 16, col_width), f32),
+            pltpu.VMEM((part_rows, 128), f32),
+            pltpu.VMEM((part_rows, 128), f32),
+            pltpu.VMEM((16, own_rows, col_width), f32),
+            pltpu.VMEM((16, own_rows, col_width), f32),
+            pltpu.VMEM((own_rows, full_cols), f32),
+            pltpu.VMEM((own_rows, head_count, head_size), f32),
+            pltpu.VMEM((own_rows, head_count, head_size), f32),
+            pltpu.VMEM((8, 16, head_width // 4), f32),
+            pltpu.VMEM((8, 16, head_width // 4), bf16),
+            pltpu.VMEM((16, 16, head_width // 4), bf16),
+            pltpu.VMEM((part_rows, head_width), f32),
+            pltpu.VMEM((part_rows, head_width), bf16),
+            pltpu.VMEM(key_cache.shape, bf16),
+            pltpu.VMEM(value_cache.shape, bf16),
+            pltpu.VMEM((8, head_width, out_cols), bf16),
+            pltpu.VMEM((8, part_rows, out_cols), f32),
+            pltpu.VMEM((4, part_rows, out_cols), f32),
+            pltpu.VMEM((3, part_rows, out_cols), f32),
+            dma((RING,)), dma((2,)), dma((8,)), dma((8,)), dma((8,)), dma, dma,
+            dma((16,)), dma((16,)), dma((16,)), dma((16,)),
+            dma((4,)), dma((4,)), dma((3,)), dma((3,)),
+        ],
+        compiler_params=pltpu.CompilerParams(
+            collective_id=0, has_side_effects=True, vmem_limit_bytes=63 * 2**20
+        ),
+        cost_estimate=pl.CostEstimate(
+            flops=2 * part_rows * (w_rows * col_width + head_width * out_width),
+            bytes_accessed=2 * (w_rows * col_width + head_width * out_width),
+            transcendentals=0,
+        ),
+        name="attention_block",
+    )(
+        hidden_in, jnp.cos(angle_now), jnp.sin(angle_now), spread,
+        w_qkv, w_out, key_cache, value_cache,
+    )
+
+
 def solution(mesh):
     placed = (
         P("groups", "mp"),

time: 242 us -> 102 us (0.42)
  waiting for transfers between devices: 107 us -> 0 us
  blocking collectives: 61.2 us -> 0 us
  Pallas kernels: 0 us -> 60.8 us
  matrix products: 43.1 us -> 0 us
  local copies, waits for them, and re-layouts: 3.98 us -> 38.5 us
  between operations: 13.7 us -> 0.01 us
  starting transfers between devices: 9.37 us -> 0 us
  other arithmetic: 3.94 us -> 1.36 us
    ppermute x10 -> x0, waiting for transfers between devices: 69.7 us -> none  [swapped(): return lax.ppermute(value, axis, pairs)]
    psum x1 -> x0, blocking collectives: 61.2 us -> none  [shards(): lax.psum((sums_local, squares_local, columns_local), 'mp')]
    pallas_call x0 -> x1, Pallas kernels: none -> 60.8 us  [shards(): pl.pallas_call(block_kernel, out_shape=jax.ShapeDtypeStruct((part_rows, o...]
    dot_general x5 -> x0, matrix products: 43.1 us -> none  [the longest x1 13.8 us: shards(): jnp.dot(feature_block, qkv_tile, preferred_element_type=jnp.float32)]
    all_gather x1 -> x0, waiting for transfers between devices: 37.1 us -> none  [shards(): lax.all_gather(attended, 'mp', axis=0, tiled=True)]
    unnamed x9 -> x2, local copies, waits for them, and re-layouts: 3.43 us -> 37.3 us
    ppermute x10 -> x0, starting transfers between devices: 9.37 us -> none  [swapped(): return lax.ppermute(value, axis, pairs)]
  transfers between devices with their start and end apart: 11 -> 0, of which waited for: 9 -> 0; matrix products, arithmetic and copies ran while one was open for 6% -> 0% of each run, Pallas kernels for 0% -> 0%
where the time goes in v1:
time: 102 us; the launch traced here: 101 us
  Pallas kernels  60.8 us (60%)
  local copies, waits for them, and re-layouts  38.5 us (38%)
  other arithmetic  1.36 us (1%)
    pallas_call x1, Pallas kernels, shards(): pl.pallas_call(block_kernel, out_shape=jax.ShapeDtypeStruct((part_rows, o...  60.8 us
    unnamed x2, local copies, waits for them, and re-layouts  37.3 us

profile of v1, /device:TPU:0, one launch (start us, length us, event | category | flops | bytes accessed | tf_op | source)
XLA Modules:
  0.0 100.7 jit_solution(7652639076370835917)
XLA Ops:
  0.0 0.7 convert_element_type.3
  0.7 1.3 %broadcast_in_dim.2.len_ref = s32[4,128]{1,0:T(4,128)} broadcast(s32[4]{0:T(128)} %param.11), dimensions={0} | broadcast | bytes 2064 | tf_op jit(solution)/shard_map/broadcast_in_dim | solution.py:476
  1.9 0.7 multiply_sine_fusion
  2.6 35.7 %copy.7.wq_hbm = bf16[1,9216,1600]{2,1,0:T(8,128)(2,1)} copy(bf16[1,9216,1600]{1,2,0:T(8,128)(2,1)} %param.7) | data formatting | bytes 58982400 | tf_op args[1]
  38.3 60.8 %attention_block.1 = bf16[64,1152]{1,0:T(8,128)(2,1)} custom-call(bf16[64,1152]{1,0:T(8,128)(2,1)} %hid_ref.1, f32[4,128]{1,0:T(4,128)} %get-tuple-element.6.cos_ref, f32[4,128]{1,0:T(4,128)} %get-tuple-element.5.sin_ref, s32[4,128]{1,0:T(4,128)} %broadcast_in_dim.2.len_ref, bf16[1,9216,1600]{2,1,0:T(8,128)(2,1)} %copy.7.wq_hbm, ...), custom_call_target="tpu_custom_call" | custom-call | flops 3699376128 | bytes 57802752 | tf_op jit(solution)/shard_map/attention_block/pallas_call | solution.py:481
  99.1 1.6 %copy.9 = bf16[64,1152]{1,0:T(8,128)(2,1)} copy(bf16[64,1152]{1,0:T(8,128)(2,1)} %attention_block.1) | data formatting | bytes 294912
  (1 shorter events, 0.0 us)

commit v2 on v1

--- a/solution.py
+++ b/solution.py
@@ -1,5 +1,6 @@
 import jax
 import jax.numpy as jnp
+import numpy as np
 from jax import lax
 from jax.experimental import pallas as pl
 from jax.experimental.pallas import tpu as pltpu
@@ -177,7 +178,7 @@
     return outputs.astype(jnp.bfloat16)
 
 
-RING = 4
+RING = 8
 
 
 def flipped(index, flips, bits):
@@ -190,9 +191,9 @@
 
 
 def block_kernel(
-    hid_ref, cos_ref, sin_ref, len_ref, wq_hbm, wo_hbm, key_hbm, val_hbm, out_ref,
-    xb, wb, acc, stat_send, stat_recv, psb, prb, pj, qf, attf, msgf, dsb, drb, lhsf, lhs,
-    keys, vals, wo, pbuf, erecv, irecv,
+    hid_ref, freq_ref, len_ref, wq_hbm, wo_hbm, key_hbm, val_hbm, out_ref,
+    xb, wb, acc0, acc1, stat_send, stat_recv, psb0, psb1, prb0, prb1, pj, qf, attf, msgf, dsb, drb, lhsf, lhs,
+    keys, vals, wo, pbuf, erecv, isend, irecv,
     w_sem, kv_sem, wo_sem, xs_sem, xr_sem, ss_sem, sr_sem, ps_sem, pr_sem,
     ds_sem, dr_sem, es_sem, er_sem, is_sem, ir_sem,
 ):
@@ -200,8 +201,10 @@
     low = me % 8
     high = me // 8 * 8
     part_rows, feats = hid_ref.shape
-    own_rows = cos_ref.shape[0]
-    col_width = acc.shape[1]
+    own_rows = len_ref.shape[0]
+    halves = ((acc0, psb0, prb0), (acc1, psb1, prb1))
+    starts = (0, acc0.shape[1])
+    col_width = acc0.shape[1] + acc1.shape[1]
     head_size = qf.shape[2]
     head_count = qf.shape[1]
     half_dim = head_size // 2
@@ -209,9 +212,14 @@
     out_cols = wo.shape[2]
     n_dev = 16
 
-    def w_copy(step, slot):
-        rows = pl.ds(pl.multiple_of(flipped(low, step, 3) * feats, feats), feats)
-        return pltpu.make_async_copy(wq_hbm.at[0, rows], wb.at[slot], w_sem.at[slot])
+    def w_copy(half, step):
+        cols = pl.ds(pl.multiple_of(flipped(low, step, 3) * feats, feats), feats)
+        count = halves[half][0].shape[1]
+        return pltpu.make_async_copy(
+            wq_hbm.at[0, pl.ds(starts[half], count), cols],
+            wb.at[step, pl.ds(0, count)],
+            w_sem.at[half, step],
+        )
 
     def wo_copy(block):
         cols = pl.ds(block * out_cols, out_cols)
@@ -221,13 +229,15 @@
     val_copy = pltpu.make_async_copy(val_hbm, vals, kv_sem.at[1])
 
     for step in range(RING):
-        w_copy(step, step).start()
+        w_copy(0, step).start()
 
     barrier = pltpu.get_barrier_semaphore()
     for flips in range(1, n_dev):
         pl.semaphore_signal(
             barrier, inc=1, device_id={"mp": flipped(me, flips, 4)}, device_id_type=MESH
         )
+    angle_now = len_ref[...].astype(jnp.float32) * freq_ref[...]
+    cosines, sines = jnp.cos(angle_now), jnp.sin(angle_now)
     pl.semaphore_wait(barrier, n_dev - 1)
 
     def x_copy(source, flips, slot):
@@ -240,16 +250,27 @@
     for flips in (2, 4, 6, 1):
         x_copy(hid_ref, flips, flips).start()
     xb[0] = hid_ref[...]
-    acc[...] = jnp.zeros_like(acc)
+    acc0[...] = jnp.zeros_like(acc0)
+    acc1[...] = jnp.zeros_like(acc1)
 
     stat_copy = pltpu.make_async_remote_copy(
         src_ref=stat_send, dst_ref=stat_recv, send_sem=ss_sem, recv_sem=sr_sem,
         device_id={"mp": flipped(me, 8, 4)}, device_id_type=MESH,
     )
 
-    def step_body(step, sums):
+    def multiply(half, step):
+        total = halves[half][0]
+        w_copy(half, step).wait()
+        with_ones = jnp.concatenate([xb[step], jnp.ones((16, feats), jnp.bfloat16)], 0)
+        total[...] += lax.dot_general(
+            with_ones,
+            wb[step, : total.shape[1]],
+            (((1,), (1,)), ((), ())),
+            preferred_element_type=jnp.float32,
+        )
+
+    def first_body(step, sums):
         total, squares = sums
-        slot = step % RING
 
         @pl.when(step > 0)
         def _():
@@ -259,8 +280,7 @@
         def _():
             x_copy(xb.at[step], 1, step + 1).start()
 
-        features = xb[step]
-        wide = features.astype(jnp.float32)
+        wide = xb[step].astype(jnp.float32)
         total = total + jnp.sum(wide, 1, keepdims=True)
         squares = squares + jnp.sum(wide * wide, 1, keepdims=True)
 
@@ -270,60 +290,70 @@
             stat_send[...] = jnp.where(lane < 64, total, squares)
             stat_copy.start()
 
-        w_copy(step, slot).wait()
-        with_ones = jnp.concatenate([features, jnp.ones((16, feats), jnp.bfloat16)], 0)
-        acc[...] += jnp.dot(with_ones, wb[slot], preferred_element_type=jnp.float32)
-
-        @pl.when(step + RING < 8)
-        def _():
-            w_copy(step + RING, slot).start()
-
-        @pl.when(step == 3)
+        multiply(0, step)
+        w_copy(1, step).start()
+        return (total, squares)
+
+    def p_copy(half, flips):
+        target = flipped(me, flips, 4)
+        return pltpu.make_async_remote_copy(
+            src_ref=halves[half][1].at[target], dst_ref=halves[half][2].at[me],
+            send_sem=ps_sem.at[half, flips], recv_sem=pr_sem.at[half, flips],
+            device_id={"mp": target}, device_id_type=MESH,
+        )
+
+    def p_arrival(half, flips):
+        source = flipped(me, flips, 4)
+        return pltpu.make_async_remote_copy(
+            src_ref=halves[half][1].at[source], dst_ref=halves[half][2].at[source],
+            send_sem=ps_sem.at[half, flips], recv_sem=pr_sem.at[half, flips],
+            device_id={"mp": source}, device_id_type=MESH,
+        )
+
+    def send_half(half):
+        total, outgoing, arriving = halves[half]
+        both = stat_send[...] + stat_recv[...]
+        row_mean = both[:, :1] / D
+        variance = both[:, 64:65] / D - row_mean * row_mean
+        inverse = lax.rsqrt(variance + 1e-05)
+        projected = inverse * (total[:part_rows] - row_mean * total[part_rows : part_rows + 1])
+        for dev in range(n_dev):
+            outgoing[dev] = projected[dev * own_rows : (dev + 1) * own_rows]
+        for flips in range(n_dev - 1, 0, -1):
+            p_copy(half, flips).start()
+        arriving[me] = outgoing[me]
+
+    def second_body(step, carry):
+        multiply(1, step)
+
+        @pl.when(step == 0)
         def _():
             key_copy.start()
             val_copy.start()
             for block in range(4):
                 wo_copy(block).start()
-
-        @pl.when(step == 5)
+            stat_copy.wait()
+            send_half(0)
+
+        @pl.when(step == 3)
         def _():
             for block in range(4, 8):
                 wo_copy(block).start()
 
-        return (total, squares)
+        return carry
 
     nothing = jnp.zeros((part_rows, 1), jnp.float32)
-    lax.fori_loop(0, 8, step_body, (nothing, nothing))
-    stat_copy.wait()
-    both = stat_send[...] + stat_recv[...]
-    row_mean = both[:, :1] / D
-    variance = both[:, 64:65] / D - row_mean * row_mean
-    inverse = lax.rsqrt(variance + 1e-05)
-    projected = inverse * (acc[:part_rows] - row_mean * acc[part_rows : part_rows + 1])
-    for dev in range(n_dev):
-        psb[dev] = projected[dev * own_rows : (dev + 1) * own_rows]
-
-    def p_copy(flips):
-        target = flipped(me, flips, 4)
-        return pltpu.make_async_remote_copy(
-            src_ref=psb.at[target], dst_ref=prb.at[me], send_sem=ps_sem.at[flips],
-            recv_sem=pr_sem.at[flips], device_id={"mp": target}, device_id_type=MESH,
-        )
-
-    def p_arrival(flips):
-        source = flipped(me, flips, 4)
-        return pltpu.make_async_remote_copy(
-            src_ref=psb.at[source], dst_ref=prb.at[source], send_sem=ps_sem.at[flips],
-            recv_sem=pr_sem.at[flips], device_id={"mp": source}, device_id_type=MESH,
-        )
-
-    for flips in range(n_dev - 1, 0, -1):
-        p_copy(flips).start()
-    prb[me] = psb[me]
-    for flips in range(1, n_dev):
-        p_arrival(flips).wait_recv()
-    for block in range(8):
-        pj[:, block * col_width : (block + 1) * col_width] = prb[block] + prb[block + 8]
+    lax.fori_loop(0, 8, first_body, (nothing, nothing))
+    lax.fori_loop(0, 8, second_body, 0)
+    send_half(1)
+    for half in range(2):
+        arriving = halves[half][2]
+        count = arriving.shape[2]
+        for flips in range(1, n_dev):
+            p_arrival(half, flips).wait_recv()
+        for block in range(8):
+            first = block * col_width + starts[half]
+            pj[:, first : first + count] = arriving[block] + arriving[block + 8]
     for head in range(head_count):
         for row in range(own_rows):
             qf[row, head : head + 1, :] = pj[
@@ -339,7 +369,7 @@
         return jnp.concatenate([front * cosine - back * sine, back * cosine + front * sine], 1)
 
     for row in range(own_rows):
-        cosine, sine = cos_ref[row : row + 1], sin_ref[row : row + 1]
+        cosine, sine = cosines[row : row + 1], sines[row : row + 1]
         queries = turned(qf[row], cosine, sine).astype(jnp.bfloat16)
         new_key = turned(pj[row : row + 1, width_q : width_q + head_size], cosine, sine)
         new_key = new_key.astype(jnp.bfloat16).astype(jnp.float32)
@@ -413,7 +443,7 @@
 
     def i_copy(turn):
         return pltpu.make_async_remote_copy(
-            src_ref=pbuf.at[2 * turn + 1], dst_ref=irecv.at[turn], send_sem=is_sem.at[turn],
+            src_ref=isend.at[turn], dst_ref=irecv.at[turn], send_sem=is_sem.at[turn],
             recv_sem=ir_sem.at[turn],
             device_id={"mp": high + flipped(low, 6 - 2 * turn, 3)}, device_id_type=MESH,
         )
@@ -432,6 +462,7 @@
 
         @pl.when(turn < 3)
         def _():
+            isend[turn] = pbuf[2 * turn + 1].astype(jnp.bfloat16)
             i_copy(turn).start()
 
         return carry
@@ -439,12 +470,16 @@
     lax.fori_loop(0, 4, out_body, 0)
     for turn in range(3):
         i_copy(turn).wait_recv()
-    out_ref[...] = (pbuf[7] + irecv[0] + irecv[1] + irecv[2]).astype(jnp.bfloat16)
+    total = pbuf[7]
+    for turn in range(3):
+        total = total + irecv[turn].astype(jnp.float32)
+    out_ref[...] = total.astype(jnp.bfloat16)
 
     for slot in range(1, 8):
         x_copy(hid_ref, 1, slot).wait_send()
     for flips in range(1, n_dev):
-        p_copy(flips).wait_send()
+        p_copy(0, flips).wait_send()
+        p_copy(1, flips).wait_send()
         d_copy(flips).wait_send()
     for turn in range(4):
         e_copy(turn).wait_send()
@@ -465,14 +500,16 @@
         or feats % 128 != 0
         or head_width % 512 != 0
         or head_size != 256
+        or col_width % 64 != 0
     ):
         return shards_plain(hidden_in, w_qkv, w_out, key_cache, value_cache, lengths)
     half_dim = head_size // 2
     out_cols = out_width // 8
     full_cols = col_width * 8
     head_count = head_width * 8 // head_size
-    frequency = 10000.0 ** (-jnp.arange(half_dim, dtype=jnp.float32) / half_dim)
-    angle_now = lengths.astype(jnp.float32)[:, None] * frequency[None, :]
+    frequency = np.power(10000.0, -np.arange(half_dim) / half_dim).astype(np.float32)[None]
+    width0 = col_width // 512 * 256
+    width1 = col_width - width0
     spread = jnp.broadcast_to(lengths[:, None], (own_rows, 128))
     f32, bf16 = jnp.float32, jnp.bfloat16
     dma = pltpu.SemaphoreType.DMA
@@ -481,16 +518,19 @@
     return pl.pallas_call(
         block_kernel,
         out_shape=jax.ShapeDtypeStruct((part_rows, out_cols), bf16),
-        in_specs=[in_vmem] * 4 + [anywhere] * 4,
+        in_specs=[in_vmem] * 3 + [anywhere] * 4,
         out_specs=in_vmem,
         scratch_shapes=[
             pltpu.VMEM((8, part_rows, feats), bf16),
-            pltpu.VMEM((RING, feats, col_width), bf16),
-            pltpu.VMEM((part_rows + 16, col_width), f32),
+            pltpu.VMEM((RING, width1, feats), bf16),
+            pltpu.VMEM((part_rows + 16, width0), f32),
+            pltpu.VMEM((part_rows + 16, width1), f32),
             pltpu.VMEM((part_rows, 128), f32),
             pltpu.VMEM((part_rows, 128), f32),
-            pltpu.VMEM((16, own_rows, col_width), f32),
-            pltpu.VMEM((16, own_rows, col_width), f32),
+            pltpu.VMEM((16, own_rows, width0), f32),
+            pltpu.VMEM((16, own_rows, width1), f32),
+            pltpu.VMEM((16, own_rows, width0), f32),
+            pltpu.VMEM((16, own_rows, width1), f32),
             pltpu.VMEM((own_rows, full_cols), f32),
             pltpu.VMEM((own_rows, head_count, head_size), f32),
             pltpu.VMEM((own_rows, head_count, head_size), f32),
@@ -504,9 +544,10 @@
             pltpu.VMEM((8, head_width, out_cols), bf16),
             pltpu.VMEM((8, part_rows, out_cols), f32),
             pltpu.VMEM((4, part_rows, out_cols), f32),
-            pltpu.VMEM((3, part_rows, out_cols), f32),
-            dma((RING,)), dma((2,)), dma((8,)), dma((8,)), dma((8,)), dma, dma,
-            dma((16,)), dma((16,)), dma((16,)), dma((16,)),
+            pltpu.VMEM((3, part_rows, out_cols), bf16),
+            pltpu.VMEM((3, part_rows, out_cols), bf16),
+            dma((2, RING)), dma((2,)), dma((8,)), dma((8,)), dma((8,)), dma, dma,
+            dma((2, 16)), dma((2, 16)), dma((16,)), dma((16,)),
             dma((4,)), dma((4,)), dma((3,)), dma((3,)),
         ],
         compiler_params=pltpu.CompilerParams(
@@ -519,8 +560,8 @@
         ),
         name="attention_block",
     )(
-        hidden_in, jnp.cos(angle_now), jnp.sin(angle_now), spread,
-        w_qkv, w_out, key_cache, value_cache,
+        hidden_in, jnp.asarray(frequency), spread,
+        jnp.swapaxes(w_qkv, 1, 2), w_out, key_cache, value_cache,
     )
 
 

time: 102 us -> 57.6 us (0.56); the launches traced: 101 us -> 57.5 us
  local copies, waits for them, and re-layouts: 38.5 us -> 2.88 us
  Pallas kernels: 60.8 us -> 54.6 us
  other arithmetic: 1.36 us -> 0 us
    unnamed x2 -> x1, local copies, waits for them, and re-layouts: 37.3 us -> 1.58 us
    pallas_call x1, Pallas kernels: 60.8 us -> 54.6 us  [shards(): pl.pallas_call(block_kernel, out_shape=jax.ShapeDtypeStruct((part_rows, o...]
where the time goes in v2:
time: 57.6 us; the launch traced here: 57.5 us
  Pallas kernels  54.6 us (95%)
  local copies, waits for them, and re-layouts  2.88 us (5%)
    pallas_call x1, Pallas kernels, shards(): pl.pallas_call(block_kernel, out_shape=jax.ShapeDtypeStruct((part_rows, o...  54.6 us
    unnamed x1, local copies, waits for them, and re-layouts  1.58 us
    broadcast_in_dim x1, local copies, waits for them, and re-layouts, shards(): spread = jnp.broadcast_to(lengths[:, None], (own_rows, 128))  1.3 us

profile of v2, /device:TPU:0, one launch (start us, length us, event | category | flops | bytes accessed | tf_op | source)
XLA Modules:
  0.0 57.5 jit_solution(2043926356416008551)
XLA Ops:
  0.0 1.3 %broadcast_in_dim.2.len_ref = s32[4,128]{1,0:T(4,128)} broadcast(s32[4]{0:T(128)} %param.12), dimensions={0} | broadcast | bytes 2064 | tf_op jit(solution)/shard_map/broadcast_in_dim | solution.py:513
  1.3 54.6 %attention_block.1 = bf16[64,1152]{1,0:T(8,128)(2,1)} custom-call(bf16[64,1152]{1,0:T(8,128)(2,1)} %hid_ref.1, f32[1,128]{1,0:T(1,128)} %constant.2.clone.freq_ref, s32[4,128]{1,0:T(4,128)} %broadcast_in_dim.2.len_ref, bf16[1,1600,9216]{2,1,0:T(8,128)(2,1)} %bitcast.1, bf16[1,1536,9216]{2,1,0:T(8,128)(2,1)} %wo_hbm.1, bf16[4,1792,256]{2,1,0:T(8,128)(2,1)} %key_hbm.1, ...), custom_call_target="tpu_custom_call" | custom-call | flops 3699376128 | bytes 57802752 | tf_op jit(solution)/shard_map/attention_block/pallas_call | solution.py:518
  55.9 1.6 %copy.9 = bf16[64,1152]{1,0:T(8,128)(2,1)} copy(bf16[64,1152]{1,0:T(8,128)(2,1)} %attention_block.1) | data formatting | bytes 294912

commit v3 on v2

--- a/solution.py
+++ b/solution.py
@@ -230,13 +230,17 @@
 
     for step in range(RING):
         w_copy(0, step).start()
+    key_copy.start()
+    val_copy.start()
 
     barrier = pltpu.get_barrier_semaphore()
     for flips in range(1, n_dev):
         pl.semaphore_signal(
             barrier, inc=1, device_id={"mp": flipped(me, flips, 4)}, device_id_type=MESH
         )
-    angle_now = len_ref[...].astype(jnp.float32) * freq_ref[...]
+    angle_now = jnp.concatenate(
+        [len_ref[row].astype(jnp.float32) * freq_ref[...] for row in range(own_rows)], 0
+    )
     cosines, sines = jnp.cos(angle_now), jnp.sin(angle_now)
     pl.semaphore_wait(barrier, n_dev - 1)
 
@@ -249,6 +253,8 @@
 
     for flips in (2, 4, 6, 1):
         x_copy(hid_ref, flips, flips).start()
+    for block in range(8):
+        wo_copy(block).start()
     xb[0] = hid_ref[...]
     acc0[...] = jnp.zeros_like(acc0)
     acc1[...] = jnp.zeros_like(acc1)
@@ -328,17 +334,8 @@
 
         @pl.when(step == 0)
         def _():
-            key_copy.start()
-            val_copy.start()
-            for block in range(4):
-                wo_copy(block).start()
             stat_copy.wait()
             send_half(0)
-
-        @pl.when(step == 3)
-        def _():
-            for block in range(4, 8):
-                wo_copy(block).start()
 
         return carry
 
@@ -379,7 +376,7 @@
             queries, keys[row], (((1,), (1,)), ((), ())), preferred_element_type=jnp.float32
         )
         slots = lax.broadcasted_iota(jnp.int32, scores.shape, 1)
-        scores = jnp.where(slots < len_ref[row : row + 1, :1], scores, -1e30)
+        scores = jnp.where(slots < len_ref[row], scores, -1e30)
         own_score = scale * jnp.sum(queries.astype(jnp.float32) * new_key, 1, keepdims=True)
         largest = jnp.maximum(jnp.max(scores, 1, keepdims=True), own_score)
         weights = jnp.exp(scores - largest)
@@ -510,7 +507,6 @@
     frequency = np.power(10000.0, -np.arange(half_dim) / half_dim).astype(np.float32)[None]
     width0 = col_width // 512 * 256
     width1 = col_width - width0
-    spread = jnp.broadcast_to(lengths[:, None], (own_rows, 128))
     f32, bf16 = jnp.float32, jnp.bfloat16
     dma = pltpu.SemaphoreType.DMA
     in_vmem = pl.BlockSpec(memory_space=pltpu.VMEM)
@@ -518,7 +514,7 @@
     return pl.pallas_call(
         block_kernel,
         out_shape=jax.ShapeDtypeStruct((part_rows, out_cols), bf16),
-        in_specs=[in_vmem] * 3 + [anywhere] * 4,
+        in_specs=[in_vmem, in_vmem, pl.BlockSpec(memory_space=pltpu.SMEM)] + [anywhere] * 4,
         out_specs=in_vmem,
         scratch_shapes=[
             pltpu.VMEM((8, part_rows, feats), bf16),
@@ -560,7 +556,7 @@
         ),
         name="attention_block",
     )(
-        hidden_in, jnp.asarray(frequency), spread,
+        hidden_in, jnp.asarray(frequency), lengths,
         jnp.swapaxes(w_qkv, 1, 2), w_out, key_cache, value_cache,
     )
 

time: 57.6 us -> 57 us (0.990)
  local copies, waits for them, and re-layouts: 2.88 us -> 1.58 us
  Pallas kernels: 54.6 us -> 55.3 us
    broadcast_in_dim x1 -> x0, local copies, waits for them, and re-layouts: 1.3 us -> none  [shards(): spread = jnp.broadcast_to(lengths[:, None], (own_rows, 128))]
    pallas_call x1, Pallas kernels: 54.6 us -> 55.3 us  [shards(): pl.pallas_call(block_kernel, out_shape=jax.ShapeDtypeStruct((part_rows, o...]
where the time goes in v3:
time: 57 us; the launch traced here: 56.9 us
  Pallas kernels  55.3 us (97%)
  local copies, waits for them, and re-layouts  1.58 us (3%)
    pallas_call x1, Pallas kernels, shards(): pl.pallas_call(block_kernel, out_shape=jax.ShapeDtypeStruct((part_rows, o...  55.3 us
    unnamed x1, local copies, waits for them, and re-layouts  1.58 us

profile of v3, /device:TPU:0, one launch (start us, length us, event | category | flops | bytes accessed | tf_op | source)
XLA Modules:
  0.0 56.9 jit_solution(14478997443817946028)
XLA Ops:
  0.0 55.3 %attention_block.1 = bf16[64,1152]{1,0:T(8,128)(2,1)} custom-call(bf16[64,1152]{1,0:T(8,128)(2,1)} %hid_ref.1, f32[1,128]{1,0:T(1,128)} %constant.2.clone.freq_ref, s32[4]{0:T(128)} %len_ref.1, bf16[1,1600,9216]{2,1,0:T(8,128)(2,1)} %bitcast.1, bf16[1,1536,9216]{2,1,0:T(8,128)(2,1)} %wo_hbm.1, bf16[4,1792,256]{2,1,0:T(8,128)(2,1)} %key_hbm.1, ...), custom_call_target="tpu_custom_call" | custom-call | flops 3699376128 | bytes 57802752 | tf_op jit(solution)/shard_map/attention_block/pallas_call | solution.py:514
  55.3 1.6 %copy.9 = bf16[64,1152]{1,0:T(8,128)(2,1)} copy(bf16[64,1152]{1,0:T(8,128)(2,1)} %attention_block.1) | data formatting | bytes 294912
